TPU v7x, 32 devices: a whole 2x2x4 slice. The times are simulated.
32 devices in a mesh: groups: 2 (over y), blk: 16 (over z, x, core).
Axes of the slice: x: 2, y: 2, z: 4, core: 2. Of those that a mesh axis runs over, the one named last changes fastest.
Arguments:
- particles: bfloat16 [16384, 256], P(('groups', 'blk')), parts along dimension 0
- class_ids: int32 [16384], P(('groups', 'blk')), parts along dimension 0, may hold values from 0 to 63
- score_table: float32 [64, 256], replicated, may hold values from -18 to 18
- precision: float32 [256], replicated, may hold values from 0.3 to 3
- plan: int32 [4, 16], replicated, may hold values from 0 to 15, as said below
- median: float32 [2], P('groups'), parts along dimension 0, may hold values from 20.364676 to 24.89016
Outputs:
- drift: float32 [16384, 256], P(('groups', 'blk')), parts along dimension 0
There are 2 independent parts, one for each index of `groups`. A program takes and returns all parts, laid end to end along the dimension named above; an argument that names none is the same for every part. Nothing has to cross between parts.
Inputs may be any that keep to these rules, and one draw needn't show every extreme that they name: `plan`: row r maps each block b to b xor m_r, where m_r is a power of two; the m_r of different rows differ.
All inputs are finite; a program needn't handle non-finite values.
Results may differ from a plain program's by a relative error of at most 0.0021.
Values may be sent and summed in bfloat16 or wider, within the bound.
A program may use at most 64 MiB of HBM per device.

v0:
```python
import math

import jax
import jax.numpy as jnp
from jax import lax
from jax.sharding import PartitionSpec as P

ROUNDS = 4


def for_sending(array):
    return jax.tree.map(lambda a: a.astype(jnp.bfloat16) if a.dtype == jnp.float32 else a, array)


def swapped(array, axis, stride):
    return lax.ppermute(array, axis, [(i, i ^ 1 << stride) for i in range(lax.axis_size(axis))])


def scores_of(ids, points, table, precision):
    classes = table.shape[0]
    onehot = (ids[:, None] == jnp.arange(classes, dtype=jnp.int32)[None, :]).astype(jnp.float32)
    looked = jnp.dot(
        onehot, table, precision=lax.Precision.HIGHEST, preferred_element_type=jnp.float32
    )
    return (looked - precision[None, :] * points.astype(jnp.float32)).astype(jnp.bfloat16)


def tile_terms(left, right, right_scores, inv_t):
    gram = lax.dot_general(
        left, right, (((1,), (1,)), ((), ())), preferred_element_type=jnp.float32
    )
    left_wide = left.astype(jnp.float32)
    right_wide = right.astype(jnp.float32)
    squared = (
        jnp.sum(left_wide * left_wide, axis=1)[:, None]
        + jnp.sum(right_wide * right_wide, axis=1)[None, :]
        - 2.0 * gram
    )
    kernel = jnp.exp(-squared * inv_t).astype(jnp.bfloat16)
    kernel = lax.optimization_barrier(kernel)
    mass = jnp.sum(kernel.astype(jnp.float32), axis=1, keepdims=True)
    weighted = jnp.dot(kernel, right_scores, preferred_element_type=jnp.float32)
    moved = jnp.dot(kernel, right, preferred_element_type=jnp.float32)
    repulse = 2.0 * inv_t * (left_wide * mass - moved)
    return (mass, weighted, repulse)


def hop_every(payload, distance, bit):
    flag = jnp.bitwise_and(jnp.right_shift(distance, bit), 1)
    arrived = jax.tree.map(
        lambda part, own: part.astype(own.dtype), swapped(for_sending(payload), "blk", bit), payload
    )
    return tuple((jnp.where(flag == 1, fresh, stale) for fresh, stale in zip(arrived, payload)))


def per_device(particles, class_ids, score_table, precision, plan, median):
    rows = particles.shape[0]
    nbits = lax.axis_size("blk").bit_length() - 1
    inv_h = jnp.float32(math.log(1.0 + (ROUNDS + 1) * rows)) / (median[0] * median[0])
    scores = scores_of(class_ids, particles, score_table, precision)
    mass, weighted, repulse = tile_terms(particles, particles, scores, inv_h)
    order_bits = list(range(nbits))
    for step in range(ROUNDS):
        distance = plan[step, 0]
        payload = (particles, scores)
        for bit in order_bits:
            payload = hop_every(payload, distance, bit)
        partner_points, partner_scores = payload
        m, w, p = tile_terms(
            particles, partner_points, partner_scores, inv_h / jnp.float32(step + 1)
        )
        mass = mass + m
        weighted = weighted + w
        repulse = repulse + p
    return (weighted + repulse) / mass


def solution(mesh):
    placed = (P(("groups", "blk"), None), P(("groups", "blk")), P(), P(), P(), P("groups"))
    return jax.shard_map(
        per_device,
        mesh=mesh,
        in_specs=placed,
        out_specs=P(("groups", "blk"), None),
        check_vma=False,
    )
```

profile of v0, /device:TPU:0, one launch (start us, length us, event | category | flops | bytes accessed | tf_op | source)
XLA Modules:
  0.0 175.4 jit_solution(3502078689589434418)
XLA Ops:
  0.8 1.4 fusion.41
  2.2 0.5 collective-permute-start.4
  4.2 0.5 copy-done.2
  4.7 0.6 fusion.54
  8.2 2.6 %collective-permute-start.20 = (bf16[512,256]{1,0:T(8,128)(2,1)S(1)}, bf16[512,256]{1,0:T(8,128)(2,1)}, u32[]{:S(2)}, u32[]{:S(2)}) collective-permute-start(bf16[512,256]{1,0:T(8,128)(2,1)S(1)} %get-tuple-element.18), channel_id=1, source_target_pairs={{0,2},{1,3},{2,0},{3,1},{4,6},{5,7},{6,4},{7,5},{8,10},{9,11},{10,... | collective-permute-start | bytes 786440 | tf_op jit(solution)/shard_map/ppermute | solution.py:16
  18.8 2.1 %collective-permute-start.14 = (bf16[512,256]{1,0:T(8,128)(2,1)S(1)}, bf16[512,256]{1,0:T(8,128)(2,1)S(1)}, u32[]{:S(2)}, u32[]{:S(2)}) collective-permute-start(bf16[512,256]{1,0:T(8,128)(2,1)S(1)} %get-tuple-element.19), channel_id=1, source_target_pairs={{0,2},{1,3},{2,0},{3,1},{4,6},{5,7},{6,4},{7,5},{8,10},{9,11},{10,... | collective-permute-start | bytes 786440 | tf_op jit(solution)/shard_map/ppermute | solution.py:16
  21.0 1.9 %collective-permute-start.8 = (bf16[512,256]{1,0:T(8,128)(2,1)S(1)}, bf16[512,256]{1,0:T(8,128)(2,1)S(1)}, u32[]{:S(2)}, u32[]{:S(2)}) collective-permute-start(bf16[512,256]{1,0:T(8,128)(2,1)S(1)} %get-tuple-element.17), channel_id=1, source_target_pairs={{0,2},{1,3},{2,0},{3,1},{4,6},{5,7},{6,4},{7,5},{8,10},{9,11},{10,... | collective-permute-start | bytes 786440 | tf_op jit(solution)/shard_map/ppermute | solution.py:16
  23.1 0.6 collective-permute-done.23
  23.7 1.9 %collective-permute-start.5 = (bf16[512,256]{1,0:T(8,128)(2,1)S(1)}, bf16[512,256]{1,0:T(8,128)(2,1)S(1)}, u32[]{:S(2)}, u32[]{:S(2)}) collective-permute-start(bf16[512,256]{1,0:T(8,128)(2,1)S(1)} %get-tuple-element.16), channel_id=1, source_target_pairs={{0,2},{1,3},{2,0},{3,1},{4,6},{5,7},{6,4},{7,5},{8,10},{9,11},{10,... | collective-permute-start | bytes 786440 | tf_op jit(solution)/shard_map/ppermute | solution.py:16
  25.7 3.5 %collective-permute-done.14 = bf16[512,256]{1,0:T(8,128)(2,1)S(1)} collective-permute-done((bf16[512,256]{1,0:T(8,128)(2,1)S(1)}, bf16[512,256]{1,0:T(8,128)(2,1)S(1)}, u32[]{:S(2)}, u32[]{:S(2)}) %collective-permute-start.14) | collective-permute-done | bytes 262176 | tf_op jit(solution)/shard_map/ppermute | solution.py:16
  29.2 1.9 %collective-permute-start.11 = (bf16[512,256]{1,0:T(8,128)(2,1)S(1)}, bf16[512,256]{1,0:T(8,128)(2,1)S(1)}, u32[]{:S(2)}, u32[]{:S(2)}) collective-permute-start(bf16[512,256]{1,0:T(8,128)(2,1)S(1)} %get-tuple-element.13), channel_id=1, source_target_pairs={{0,2},{1,3},{2,0},{3,1},{4,6},{5,7},{6,4},{7,5},{8,10},{9,11},{10,... | collective-permute-start | bytes 786440 | tf_op jit(solution)/shard_map/ppermute | solution.py:16
  31.2 14.9 %collective-permute-done.17 = bf16[512,256]{1,0:T(8,128)(2,1)S(1)} collective-permute-done((bf16[512,256]{1,0:T(8,128)(2,1)S(1)}, bf16[512,256]{1,0:T(8,128)(2,1)S(1)}, u32[]{:S(2)}, u32[]{:S(2)}) %collective-permute-start.17) | collective-permute-done | bytes 262176 | tf_op jit(solution)/shard_map/ppermute | solution.py:16
  46.0 2.0 %collective-permute-start.21 = (bf16[512,256]{1,0:T(8,128)(2,1)S(1)}, bf16[512,256]{1,0:T(8,128)(2,1)S(1)}, u32[]{:S(2)}, u32[]{:S(2)}) collective-permute-start(bf16[512,256]{1,0:T(8,128)(2,1)S(1)} %broadcast_select_fusion.3), channel_id=1, source_target_pairs={{0,4},{1,5},{2,6},{3,7},{4,0},{5,1},{6,2},{7,3},{8,12},{9,13},{10,... | collective-permute-start | bytes 786440 | tf_op jit(solution)/shard_map/ppermute | solution.py:16
  48.3 2.1 %collective-permute-start.2 = (bf16[512,256]{1,0:T(8,128)(2,1)S(1)}, bf16[512,256]{1,0:T(8,128)(2,1)S(1)}, u32[]{:S(2)}, u32[]{:S(2)}) collective-permute-start(bf16[512,256]{1,0:T(8,128)(2,1)S(1)} %broadcast_select_fusion.24), channel_id=1, source_target_pairs={{0,4},{1,5},{2,6},{3,7},{4,0},{5,1},{6,2},{7,3},{8,12},{9,13},{10,... | collective-permute-start | bytes 786440 | tf_op jit(solution)/shard_map/ppermute | solution.py:16
  50.4 1.3 collective-permute-done.5
  51.7 2.0 %collective-permute-start.9 = (bf16[512,256]{1,0:T(8,128)(2,1)S(1)}, bf16[512,256]{1,0:T(8,128)(2,1)S(1)}, u32[]{:S(2)}, u32[]{:S(2)}) collective-permute-start(bf16[512,256]{1,0:T(8,128)(2,1)S(1)} %broadcast_select_fusion.17), channel_id=1, source_target_pairs={{0,4},{1,5},{2,6},{3,7},{4,0},{5,1},{6,2},{7,3},{8,12},{9,13},{10,... | collective-permute-start | bytes 786440 | tf_op jit(solution)/shard_map/ppermute | solution.py:16
  53.7 3.4 %collective-permute-done.11 = bf16[512,256]{1,0:T(8,128)(2,1)S(1)} collective-permute-done((bf16[512,256]{1,0:T(8,128)(2,1)S(1)}, bf16[512,256]{1,0:T(8,128)(2,1)S(1)}, u32[]{:S(2)}, u32[]{:S(2)}) %collective-permute-start.11) | collective-permute-done | bytes 262176 | tf_op jit(solution)/shard_map/ppermute | solution.py:16
  57.1 1.8 %collective-permute-start.24 = (bf16[512,256]{1,0:T(8,128)(2,1)S(1)}, bf16[512,256]{1,0:T(8,128)(2,1)S(1)}, u32[]{:S(2)}, u32[]{:S(2)}) collective-permute-start(bf16[512,256]{1,0:T(8,128)(2,1)S(1)} %broadcast_select_fusion.2), channel_id=1, source_target_pairs={{0,4},{1,5},{2,6},{3,7},{4,0},{5,1},{6,2},{7,3},{8,12},{9,13},{10,... | collective-permute-start | bytes 786440 | tf_op jit(solution)/shard_map/ppermute | solution.py:16
  59.3 18.5 %collective-permute-done.24 = bf16[512,256]{1,0:T(8,128)(2,1)S(1)} collective-permute-done((bf16[512,256]{1,0:T(8,128)(2,1)S(1)}, bf16[512,256]{1,0:T(8,128)(2,1)S(1)}, u32[]{:S(2)}, u32[]{:S(2)}) %collective-permute-start.24) | collective-permute-done | bytes 262176 | tf_op jit(solution)/shard_map/ppermute | solution.py:16
  77.7 2.1 %collective-permute-start.6 = (bf16[512,256]{1,0:T(8,128)(2,1)S(1)}, bf16[512,256]{1,0:T(8,128)(2,1)S(1)}, u32[]{:S(2)}, u32[]{:S(2)}) collective-permute-start(bf16[512,256]{1,0:T(8,128)(2,1)S(1)} %broadcast_select_fusion.23), channel_id=1, source_target_pairs={{0,4},{1,5},{2,6},{3,7},{4,0},{5,1},{6,2},{7,3},{8,12},{9,13},{10,... | collective-permute-start | bytes 786440 | tf_op jit(solution)/shard_map/ppermute | solution.py:16
  80.0 3.4 %collective-permute-done.18 = bf16[512,256]{1,0:T(8,128)(2,1)S(1)} collective-permute-done((bf16[512,256]{1,0:T(8,128)(2,1)S(1)}, bf16[512,256]{1,0:T(8,128)(2,1)S(1)}, u32[]{:S(2)}, u32[]{:S(2)}) %collective-permute-start.18) | collective-permute-done | bytes 262176 | tf_op jit(solution)/shard_map/ppermute | solution.py:16
  83.4 3.1 %collective-permute-start.22 = (bf16[512,256]{1,0:T(8,128)(2,1)S(1)}, bf16[512,256]{1,0:T(8,128)(2,1)S(1)}, u32[]{:S(2)}, u32[]{:S(2)}) collective-permute-start(bf16[512,256]{1,0:T(8,128)(2,1)S(1)} %broadcast_select_fusion.5), channel_id=1, source_target_pairs={{0,8},{1,9},{2,10},{3,11},{4,12},{5,13},{6,14},{7,15},{8,0},{9,1},... | collective-permute-start | bytes 786440 | tf_op jit(solution)/shard_map/ppermute | solution.py:16
  86.6 3.0 %collective-permute-start.3 = (bf16[512,256]{1,0:T(8,128)(2,1)S(1)}, bf16[512,256]{1,0:T(8,128)(2,1)S(1)}, u32[]{:S(2)}, u32[]{:S(2)}) collective-permute-start(bf16[512,256]{1,0:T(8,128)(2,1)S(1)} %broadcast_select_fusion.26), channel_id=1, source_target_pairs={{0,8},{1,9},{2,10},{3,11},{4,12},{5,13},{6,14},{7,15},{8,0},{9,1},... | collective-permute-start | bytes 786440 | tf_op jit(solution)/shard_map/ppermute | solution.py:16
  89.6 10.4 %collective-permute-done.6 = bf16[512,256]{1,0:T(8,128)(2,1)S(1)} collective-permute-done((bf16[512,256]{1,0:T(8,128)(2,1)S(1)}, bf16[512,256]{1,0:T(8,128)(2,1)S(1)}, u32[]{:S(2)}, u32[]{:S(2)}) %collective-permute-start.6) | collective-permute-done | bytes 262176 | tf_op jit(solution)/shard_map/ppermute | solution.py:16
  100.4 4.0 %collective-permute-done.12 = bf16[512,256]{1,0:T(8,128)(2,1)S(1)} collective-permute-done((bf16[512,256]{1,0:T(8,128)(2,1)S(1)}, bf16[512,256]{1,0:T(8,128)(2,1)S(1)}, u32[]{:S(2)}, u32[]{:S(2)}) %collective-permute-start.12) | collective-permute-done | bytes 262176 | tf_op jit(solution)/shard_map/ppermute | solution.py:16
  104.4 3.0 %collective-permute-start.19 = (bf16[512,256]{1,0:T(8,128)(2,1)S(1)}, bf16[512,256]{1,0:T(8,128)(2,1)S(1)}, u32[]{:S(2)}, u32[]{:S(2)}) collective-permute-start(bf16[512,256]{1,0:T(8,128)(2,1)S(1)} %broadcast_select_fusion.11), channel_id=1, source_target_pairs={{0,8},{1,9},{2,10},{3,11},{4,12},{5,13},{6,14},{7,15},{8,0},{9,1},... | collective-permute-start | bytes 786440 | tf_op jit(solution)/shard_map/ppermute | solution.py:16
  108.0 25.0 %collective-permute-done.16 = bf16[512,256]{1,0:T(8,128)(2,1)S(1)} collective-permute-done((bf16[512,256]{1,0:T(8,128)(2,1)S(1)}, bf16[512,256]{1,0:T(8,128)(2,1)S(1)}, u32[]{:S(2)}, u32[]{:S(2)}) %collective-permute-start.16) | collective-permute-done | bytes 262176 | tf_op jit(solution)/shard_map/ppermute | solution.py:16
  133.9 7.5 %collective-permute-done.3 = bf16[512,256]{1,0:T(8,128)(2,1)S(1)} collective-permute-done((bf16[512,256]{1,0:T(8,128)(2,1)S(1)}, bf16[512,256]{1,0:T(8,128)(2,1)S(1)}, u32[]{:S(2)}, u32[]{:S(2)}) %collective-permute-start.3) | collective-permute-done | bytes 262176 | tf_op jit(solution)/shard_map/ppermute | solution.py:16
  142.5 10.1 %collective-permute-done.10 = bf16[512,256]{1,0:T(8,128)(2,1)S(1)} collective-permute-done((bf16[512,256]{1,0:T(8,128)(2,1)S(1)}, bf16[512,256]{1,0:T(8,128)(2,1)S(1)}, u32[]{:S(2)}, u32[]{:S(2)}) %collective-permute-start.10) | collective-permute-done | bytes 262176 | tf_op jit(solution)/shard_map/ppermute | solution.py:16
  154.4 17.1 %collective-permute-done.7 = bf16[512,256]{1,0:T(8,128)(2,1)S(1)} collective-permute-done((bf16[512,256]{1,0:T(8,128)(2,1)S(1)}, bf16[512,256]{1,0:T(8,128)(2,1)S(1)}, u32[]{:S(2)}, u32[]{:S(2)}) %collective-permute-start.7) | collective-permute-done | bytes 262176 | tf_op jit(solution)/shard_map/ppermute | solution.py:16
  172.5 1.9 %collective-permute-done.13 = bf16[512,256]{1,0:T(8,128)(2,1)S(1)} collective-permute-done((bf16[512,256]{1,0:T(8,128)(2,1)S(1)}, bf16[512,256]{1,0:T(8,128)(2,1)S(1)}, u32[]{:S(2)}, u32[]{:S(2)}) %collective-permute-start.13) | collective-permute-done | bytes 262176 | tf_op jit(solution)/shard_map/ppermute | solution.py:16
  174.3 1.1 fusion.40
  (72 shorter events, 9.1 us)
Async XLA Ops:
  0.0 0.8 copy-start
  0.0 2.7 %copy-start.1 = (bf16[512,256]{1,0:T(8,128)(2,1)S(1)}, bf16[512,256]{1,0:T(8,128)(2,1)}, u32[]{:S(2)}) copy-start(bf16[512,256]{1,0:T(8,128)(2,1)} %param.6) | copy-start | bytes 786436
  0.0 8.1 %collective-permute-start = (bf16[512,256]{1,0:T(8,128)(2,1)}, bf16[512,256]{1,0:T(8,128)(2,1)S(1)}, u32[]{:S(2)}, u32[]{:S(2)}) collective-permute-start(bf16[512,256]{1,0:T(8,128)(2,1)} %param.6), channel_id=1, source_target_pairs={{0,1},{1,0},{2,3},{3,2},{4,5},{5,4},{6,7},{7,6},{8,9},{9,8},{10,11... | collective-permute-start | bytes 786440 | tf_op jit(solution)/shard_map/ppermute | solution.py:16
  2.2 8.6 %collective-permute-start.4 = (bf16[512,256]{1,0:T(8,128)(2,1)S(1)}, bf16[512,256]{1,0:T(8,128)(2,1)S(1)}, u32[]{:S(2)}, u32[]{:S(2)}) collective-permute-start(bf16[512,256]{1,0:T(8,128)(2,1)S(1)} %fusion.41), channel_id=1, source_target_pairs={{0,1},{1,0},{2,3},{3,2},{4,5},{5,4},{6,7},{7,6},{8,9},{9,8},{10,11... | collective-permute-start | bytes 786440 | tf_op jit(solution)/shard_map/ppermute | solution.py:16
  4.0 0.7 copy-start.2
  8.2 14.7 %collective-permute-start.20 = (bf16[512,256]{1,0:T(8,128)(2,1)S(1)}, bf16[512,256]{1,0:T(8,128)(2,1)}, u32[]{:S(2)}, u32[]{:S(2)}) collective-permute-start(bf16[512,256]{1,0:T(8,128)(2,1)S(1)} %get-tuple-element.18), channel_id=1, source_target_pairs={{0,2},{1,3},{2,0},{3,1},{4,6},{5,7},{6,4},{7,5},{8,10},{9,11},{10,... | collective-permute-start | bytes 786440 | tf_op jit(solution)/shard_map/ppermute | solution.py:16
  10.9 12.8 %collective-permute-start.23 = (bf16[512,256]{1,0:T(8,128)(2,1)S(1)}, bf16[512,256]{1,0:T(8,128)(2,1)}, u32[]{:S(2)}, u32[]{:S(2)}) collective-permute-start(bf16[512,256]{1,0:T(8,128)(2,1)S(1)} %get-tuple-element.14), channel_id=1, source_target_pairs={{0,2},{1,3},{2,0},{3,1},{4,6},{5,7},{6,4},{7,5},{8,10},{9,11},{10,... | collective-permute-start | bytes 786440 | tf_op jit(solution)/shard_map/ppermute | solution.py:16
  18.8 10.3 %collective-permute-start.14 = (bf16[512,256]{1,0:T(8,128)(2,1)S(1)}, bf16[512,256]{1,0:T(8,128)(2,1)S(1)}, u32[]{:S(2)}, u32[]{:S(2)}) collective-permute-start(bf16[512,256]{1,0:T(8,128)(2,1)S(1)} %get-tuple-element.19), channel_id=1, source_target_pairs={{0,2},{1,3},{2,0},{3,1},{4,6},{5,7},{6,4},{7,5},{8,10},{9,11},{10,... | collective-permute-start | bytes 786440 | tf_op jit(solution)/shard_map/ppermute | solution.py:16
  20.9 27.2 %collective-permute-start.1 = (bf16[512,256]{1,0:T(8,128)(2,1)S(1)}, bf16[512,256]{1,0:T(8,128)(2,1)S(1)}, u32[]{:S(2)}, u32[]{:S(2)}) collective-permute-start(bf16[512,256]{1,0:T(8,128)(2,1)S(1)} %get-tuple-element.20), channel_id=1, source_target_pairs={{0,2},{1,3},{2,0},{3,1},{4,6},{5,7},{6,4},{7,5},{8,10},{9,11},{10,... | collective-permute-start | bytes 786440 | tf_op jit(solution)/shard_map/ppermute | solution.py:16
  21.0 27.3 %collective-permute-start.8 = (bf16[512,256]{1,0:T(8,128)(2,1)S(1)}, bf16[512,256]{1,0:T(8,128)(2,1)S(1)}, u32[]{:S(2)}, u32[]{:S(2)}) collective-permute-start(bf16[512,256]{1,0:T(8,128)(2,1)S(1)} %get-tuple-element.17), channel_id=1, source_target_pairs={{0,2},{1,3},{2,0},{3,1},{4,6},{5,7},{6,4},{7,5},{8,10},{9,11},{10,... | collective-permute-start | bytes 786440 | tf_op jit(solution)/shard_map/ppermute | solution.py:16
  22.9 23.1 %collective-permute-start.17 = (bf16[512,256]{1,0:T(8,128)(2,1)S(1)}, bf16[512,256]{1,0:T(8,128)(2,1)S(1)}, u32[]{:S(2)}, u32[]{:S(2)}) collective-permute-start(bf16[512,256]{1,0:T(8,128)(2,1)S(1)} %get-tuple-element.15), channel_id=1, source_target_pairs={{0,2},{1,3},{2,0},{3,1},{4,6},{5,7},{6,4},{7,5},{8,10},{9,11},{10,... | collective-permute-start | bytes 786440 | tf_op jit(solution)/shard_map/ppermute | solution.py:16
  23.7 28.0 %collective-permute-start.5 = (bf16[512,256]{1,0:T(8,128)(2,1)S(1)}, bf16[512,256]{1,0:T(8,128)(2,1)S(1)}, u32[]{:S(2)}, u32[]{:S(2)}) collective-permute-start(bf16[512,256]{1,0:T(8,128)(2,1)S(1)} %get-tuple-element.16), channel_id=1, source_target_pairs={{0,2},{1,3},{2,0},{3,1},{4,6},{5,7},{6,4},{7,5},{8,10},{9,11},{10,... | collective-permute-start | bytes 786440 | tf_op jit(solution)/shard_map/ppermute | solution.py:16
  29.2 27.9 %collective-permute-start.11 = (bf16[512,256]{1,0:T(8,128)(2,1)S(1)}, bf16[512,256]{1,0:T(8,128)(2,1)S(1)}, u32[]{:S(2)}, u32[]{:S(2)}) collective-permute-start(bf16[512,256]{1,0:T(8,128)(2,1)S(1)} %get-tuple-element.13), channel_id=1, source_target_pairs={{0,2},{1,3},{2,0},{3,1},{4,6},{5,7},{6,4},{7,5},{8,10},{9,11},{10,... | collective-permute-start | bytes 786440 | tf_op jit(solution)/shard_map/ppermute | solution.py:16
  46.0 12.9 %collective-permute-start.21 = (bf16[512,256]{1,0:T(8,128)(2,1)S(1)}, bf16[512,256]{1,0:T(8,128)(2,1)S(1)}, u32[]{:S(2)}, u32[]{:S(2)}) collective-permute-start(bf16[512,256]{1,0:T(8,128)(2,1)S(1)} %broadcast_select_fusion.3), channel_id=1, source_target_pairs={{0,4},{1,5},{2,6},{3,7},{4,0},{5,1},{6,2},{7,3},{8,12},{9,13},{10,... | collective-permute-start | bytes 786440 | tf_op jit(solution)/shard_map/ppermute | solution.py:16
  48.1 31.7 %collective-permute-start.15 = (bf16[512,256]{1,0:T(8,128)(2,1)S(1)}, bf16[512,256]{1,0:T(8,128)(2,1)S(1)}, u32[]{:S(2)}, u32[]{:S(2)}) collective-permute-start(bf16[512,256]{1,0:T(8,128)(2,1)S(1)} %broadcast_select_fusion.10), channel_id=1, source_target_pairs={{0,4},{1,5},{2,6},{3,7},{4,0},{5,1},{6,2},{7,3},{8,12},{9,13},{10,... | collective-permute-start | bytes 786440 | tf_op jit(solution)/shard_map/ppermute | solution.py:16
  48.3 38.2 %collective-permute-start.2 = (bf16[512,256]{1,0:T(8,128)(2,1)S(1)}, bf16[512,256]{1,0:T(8,128)(2,1)S(1)}, u32[]{:S(2)}, u32[]{:S(2)}) collective-permute-start(bf16[512,256]{1,0:T(8,128)(2,1)S(1)} %broadcast_select_fusion.24), channel_id=1, source_target_pairs={{0,4},{1,5},{2,6},{3,7},{4,0},{5,1},{6,2},{7,3},{8,12},{9,13},{10,... | collective-permute-start | bytes 786440 | tf_op jit(solution)/shard_map/ppermute | solution.py:16
  51.7 34.9 %collective-permute-start.9 = (bf16[512,256]{1,0:T(8,128)(2,1)S(1)}, bf16[512,256]{1,0:T(8,128)(2,1)S(1)}, u32[]{:S(2)}, u32[]{:S(2)}) collective-permute-start(bf16[512,256]{1,0:T(8,128)(2,1)S(1)} %broadcast_select_fusion.17), channel_id=1, source_target_pairs={{0,4},{1,5},{2,6},{3,7},{4,0},{5,1},{6,2},{7,3},{8,12},{9,13},{10,... | collective-permute-start | bytes 786440 | tf_op jit(solution)/shard_map/ppermute | solution.py:16
  57.1 20.6 %collective-permute-start.24 = (bf16[512,256]{1,0:T(8,128)(2,1)S(1)}, bf16[512,256]{1,0:T(8,128)(2,1)S(1)}, u32[]{:S(2)}, u32[]{:S(2)}) collective-permute-start(bf16[512,256]{1,0:T(8,128)(2,1)S(1)} %broadcast_select_fusion.2), channel_id=1, source_target_pairs={{0,4},{1,5},{2,6},{3,7},{4,0},{5,1},{6,2},{7,3},{8,12},{9,13},{10,... | collective-permute-start | bytes 786440 | tf_op jit(solution)/shard_map/ppermute | solution.py:16
  59.0 24.4 %collective-permute-start.18 = (bf16[512,256]{1,0:T(8,128)(2,1)S(1)}, bf16[512,256]{1,0:T(8,128)(2,1)S(1)}, u32[]{:S(2)}, u32[]{:S(2)}) collective-permute-start(bf16[512,256]{1,0:T(8,128)(2,1)S(1)} %broadcast_select_fusion.9), channel_id=1, source_target_pairs={{0,4},{1,5},{2,6},{3,7},{4,0},{5,1},{6,2},{7,3},{8,12},{9,13},{10,... | collective-permute-start | bytes 786440 | tf_op jit(solution)/shard_map/ppermute | solution.py:16
  77.7 22.3 %collective-permute-start.6 = (bf16[512,256]{1,0:T(8,128)(2,1)S(1)}, bf16[512,256]{1,0:T(8,128)(2,1)S(1)}, u32[]{:S(2)}, u32[]{:S(2)}) collective-permute-start(bf16[512,256]{1,0:T(8,128)(2,1)S(1)} %broadcast_select_fusion.23), channel_id=1, source_target_pairs={{0,4},{1,5},{2,6},{3,7},{4,0},{5,1},{6,2},{7,3},{8,12},{9,13},{10,... | collective-permute-start | bytes 786440 | tf_op jit(solution)/shard_map/ppermute | solution.py:16
  79.8 24.5 %collective-permute-start.12 = (bf16[512,256]{1,0:T(8,128)(2,1)S(1)}, bf16[512,256]{1,0:T(8,128)(2,1)S(1)}, u32[]{:S(2)}, u32[]{:S(2)}) collective-permute-start(bf16[512,256]{1,0:T(8,128)(2,1)S(1)} %broadcast_select_fusion.16), channel_id=1, source_target_pairs={{0,4},{1,5},{2,6},{3,7},{4,0},{5,1},{6,2},{7,3},{8,12},{9,13},{10,... | collective-permute-start | bytes 786440 | tf_op jit(solution)/shard_map/ppermute | solution.py:16
  83.4 21.0 %collective-permute-start.22 = (bf16[512,256]{1,0:T(8,128)(2,1)S(1)}, bf16[512,256]{1,0:T(8,128)(2,1)S(1)}, u32[]{:S(2)}, u32[]{:S(2)}) collective-permute-start(bf16[512,256]{1,0:T(8,128)(2,1)S(1)} %broadcast_select_fusion.5), channel_id=1, source_target_pairs={{0,8},{1,9},{2,10},{3,11},{4,12},{5,13},{6,14},{7,15},{8,0},{9,1},... | collective-permute-start | bytes 786440 | tf_op jit(solution)/shard_map/ppermute | solution.py:16
  86.5 46.5 %collective-permute-start.16 = (bf16[512,256]{1,0:T(8,128)(2,1)S(1)}, bf16[512,256]{1,0:T(8,128)(2,1)S(1)}, u32[]{:S(2)}, u32[]{:S(2)}) collective-permute-start(bf16[512,256]{1,0:T(8,128)(2,1)S(1)} %broadcast_select_fusion.12), channel_id=1, source_target_pairs={{0,8},{1,9},{2,10},{3,11},{4,12},{5,13},{6,14},{7,15},{8,0},{9,1},... | collective-permute-start | bytes 786440 | tf_op jit(solution)/shard_map/ppermute | solution.py:16
  86.6 54.8 %collective-permute-start.3 = (bf16[512,256]{1,0:T(8,128)(2,1)S(1)}, bf16[512,256]{1,0:T(8,128)(2,1)S(1)}, u32[]{:S(2)}, u32[]{:S(2)}) collective-permute-start(bf16[512,256]{1,0:T(8,128)(2,1)S(1)} %broadcast_select_fusion.26), channel_id=1, source_target_pairs={{0,8},{1,9},{2,10},{3,11},{4,12},{5,13},{6,14},{7,15},{8,0},{9,1},... | collective-permute-start | bytes 786440 | tf_op jit(solution)/shard_map/ppermute | solution.py:16
  100.0 52.6 %collective-permute-start.10 = (bf16[512,256]{1,0:T(8,128)(2,1)S(1)}, bf16[512,256]{1,0:T(8,128)(2,1)S(1)}, u32[]{:S(2)}, u32[]{:S(2)}) collective-permute-start(bf16[512,256]{1,0:T(8,128)(2,1)S(1)} %broadcast_select_fusion.19), channel_id=1, source_target_pairs={{0,8},{1,9},{2,10},{3,11},{4,12},{5,13},{6,14},{7,15},{8,0},{9,1},... | collective-permute-start | bytes 786440 | tf_op jit(solution)/shard_map/ppermute | solution.py:16
  104.3 67.5 %collective-permute-start.25 = (bf16[512,256]{1,0:T(8,128)(2,1)S(1)}, bf16[512,256]{1,0:T(8,128)(2,1)S(1)}, u32[]{:S(2)}, u32[]{:S(2)}) collective-permute-start(bf16[512,256]{1,0:T(8,128)(2,1)S(1)} %broadcast_select_fusion.4), channel_id=1, source_target_pairs={{0,8},{1,9},{2,10},{3,11},{4,12},{5,13},{6,14},{7,15},{8,0},{9,1},... | collective-permute-start | bytes 786440 | tf_op jit(solution)/shard_map/ppermute | solution.py:16
  104.4 67.8 %collective-permute-start.19 = (bf16[512,256]{1,0:T(8,128)(2,1)S(1)}, bf16[512,256]{1,0:T(8,128)(2,1)S(1)}, u32[]{:S(2)}, u32[]{:S(2)}) collective-permute-start(bf16[512,256]{1,0:T(8,128)(2,1)S(1)} %broadcast_select_fusion.11), channel_id=1, source_target_pairs={{0,8},{1,9},{2,10},{3,11},{4,12},{5,13},{6,14},{7,15},{8,0},{9,1},... | collective-permute-start | bytes 786440 | tf_op jit(solution)/shard_map/ppermute | solution.py:16
  133.0 38.5 %collective-permute-start.7 = (bf16[512,256]{1,0:T(8,128)(2,1)S(1)}, bf16[512,256]{1,0:T(8,128)(2,1)S(1)}, u32[]{:S(2)}, u32[]{:S(2)}) collective-permute-start(bf16[512,256]{1,0:T(8,128)(2,1)S(1)} %broadcast_select_fusion.25), channel_id=1, source_target_pairs={{0,8},{1,9},{2,10},{3,11},{4,12},{5,13},{6,14},{7,15},{8,0},{9,1},... | collective-permute-start | bytes 786440 | tf_op jit(solution)/shard_map/ppermute | solution.py:16
  141.4 32.9 %collective-permute-start.13 = (bf16[512,256]{1,0:T(8,128)(2,1)S(1)}, bf16[512,256]{1,0:T(8,128)(2,1)S(1)}, u32[]{:S(2)}, u32[]{:S(2)}) collective-permute-start(bf16[512,256]{1,0:T(8,128)(2,1)S(1)} %broadcast_select_fusion.18), channel_id=1, source_target_pairs={{0,8},{1,9},{2,10},{3,11},{4,12},{5,13},{6,14},{7,15},{8,0},{9,1},... | collective-permute-start | bytes 786440 | tf_op jit(solution)/shard_map/ppermute | solution.py:16
where the time goes:
time: 176 us; the launch traced here: 175 us
  waiting for transfers between devices  122 us (69%)
  starting transfers between devices  31.5 us (18%)
  between operations  11.2 us (6%)
  matrix products  7.46 us (4%)
  other arithmetic  2.2 us (1%)
    ppermute x26, waiting for transfers between devices, swapped(): lax.ppermute(array, axis, [(i, i ^ 1 << stride) for i in range(lax.axis_s...  122 us
    ppermute x26, starting transfers between devices, swapped(): lax.ppermute(array, axis, [(i, i ^ 1 << stride) for i in range(lax.axis_s...  31.5 us
  transfers between devices with their start and end apart: 26, of which 14 were waited for; matrix products, arithmetic and copies ran while one was open for 5% of the time, Pallas kernels for 0%

commit v1 on v0

v1 whole, which is shorter than its diff:
```python
import functools
import math

import jax
import jax.numpy as jnp
from jax import lax
from jax.experimental import pallas as pl
from jax.experimental.pallas import tpu as pltpu
from jax.sharding import PartitionSpec as P

ROUNDS = 4
CHUNKS = 2
LOG2E = math.log2(math.e)
F32, BF16 = jnp.float32, jnp.bfloat16


def flipped(index, bit):
    return index + (1 - 2 * ((index // (1 << bit)) % 2)) * (1 << bit)


def split_in_three(table):
    high = table.astype(BF16)
    rest = table - high.astype(F32)
    middle = rest.astype(BF16)
    low = (rest - middle.astype(F32)).astype(BF16)
    return jnp.concatenate([high, middle, low], axis=0)


def kernel(
    nbits,
    plan_ref,
    median_ref,
    x_hbm,
    ids_ref,
    table_ref,
    prec_ref,
    out_ref,
    own,
    slots,
    own_info,
    infos,
    norms,
    pieces,
    acc,
    mass,
    pulled,
    own_sem,
    send_sem,
    recv_sem,
    info_send,
    info_recv,
):
    rows, dims = own.shape
    size = rows // CHUNKS
    classes = table_ref.shape[0]
    me = lax.axis_index("blk")

    barrier = pltpu.get_barrier_semaphore()
    for bit in range(nbits):
        pl.semaphore_signal(
            barrier,
            inc=1,
            device_id={"blk": flipped(me, bit)},
            device_id_type=pl.DeviceIdType.MESH,
        )
    load = pltpu.make_async_copy(x_hbm, own, own_sem)
    load.start()
    pl.semaphore_wait(barrier, nbits)

    def block_copy(bit, chunk):
        part = pl.ds(chunk * size, size)
        return pltpu.make_async_remote_copy(
            src_ref=x_hbm.at[part],
            dst_ref=slots.at[bit, part],
            send_sem=send_sem.at[bit, chunk],
            recv_sem=recv_sem.at[bit, chunk],
            device_id={"blk": flipped(me, bit)},
            device_id_type=pl.DeviceIdType.MESH,
        )

    def info_copy(bit):
        return pltpu.make_async_remote_copy(
            src_ref=own_info,
            dst_ref=infos.at[bit],
            send_sem=info_send.at[bit],
            recv_sem=info_recv.at[bit],
            device_id={"blk": flipped(me, bit)},
            device_id_type=pl.DeviceIdType.MESH,
        )

    for chunk in range(CHUNKS):
        for bit in reversed(range(nbits)):
            block_copy(bit, chunk).start()

    load.wait()
    wide = own[...].astype(F32)
    half = 0.5 * jnp.sum(wide * wide, axis=1, keepdims=True)
    norms[...] = jnp.broadcast_to(half, norms.shape)
    half_row = jnp.transpose(norms[...])[0:8, :]
    ids_row = jnp.broadcast_to(ids_ref[...].astype(F32), half_row.shape)
    row = lax.broadcasted_iota(jnp.int32, half_row.shape, 0)
    own_info[...] = jnp.where(row == 0, ids_row, half_row)
    for bit in reversed(range(nbits)):
        info_copy(bit).start()

    pieces[...] = split_in_three(table_ref[...])
    acc[...] = jnp.zeros_like(acc)
    mass[...] = jnp.zeros_like(mass)
    pulled[...] = jnp.zeros_like(pulled)

    med = jnp.full((1, dims), median_ref[0], F32)
    inv_h = F32(math.log(1.0 + (ROUNDS + 1) * rows)) / (med * med)
    prec = prec_ref[...]

    def add_tile(right, info, share):
        inv = inv_h * share
        ids, half_right = info[0:1, :], info[1:2, :]
        number = lax.broadcasted_iota(jnp.int32, (classes, size), 0).astype(F32)
        onehot = jnp.transpose((number == ids).astype(F32)).astype(BF16)
        looked = jnp.dot(
            jnp.concatenate([onehot, onehot, onehot], axis=1),
            pieces[...],
            preferred_element_type=F32,
        )
        points = right.astype(F32)
        scores = (looked - prec * points).astype(BF16).astype(F32)
        pull = 2.0 * inv
        terms = (scores - pull * points).astype(BF16)
        gram = lax.dot_general(
            own[...], right, (((1,), (1,)), ((), ())), preferred_element_type=F32
        )
        left_half = jnp.concatenate([norms[...]] * (size // 128), axis=1)
        powers = ((gram - left_half) - half_right) * (pull[:, :size] * LOG2E)
        weights = jnp.exp2(powers).astype(BF16)
        acc[...] += jnp.dot(weights, terms, preferred_element_type=F32)
        wide_weights = weights.astype(F32)
        part = wide_weights[:, :128]
        for lane in range(128, size, 128):
            part = part + wide_weights[:, lane : lane + 128]
        mass[...] += part
        pulled[...] += part * pull[:, :128]

    for chunk in range(CHUNKS):
        part = pl.ds(chunk * size, size)
        add_tile(own[part, :], own_info[:, part], F32(1.0))

    def share_of_bit(bit):
        share = F32(0.0)
        for step in range(ROUNDS):
            share = jnp.where(plan_ref[step, 0] == (1 << bit), F32(1.0 / (step + 1)), share)
        return share

    if nbits == ROUNDS:
        near = min(2, nbits)
        order = [(bit, chunk) for bit in range(near) for chunk in range(CHUNKS)]
        order += [(bit, chunk) for chunk in range(CHUNKS) for bit in range(near, nbits)]
        for bit in range(near):
            info_copy(bit).wait_recv()
        for place, (bit, chunk) in enumerate(order):
            if place == near * CHUNKS:
                for later in range(near, nbits):
                    info_copy(later).wait_recv()
            block_copy(bit, chunk).wait_recv()
            part = pl.ds(chunk * size, size)
            add_tile(slots[bit, part, :], infos[bit, :, part], share_of_bit(bit))
    else:
        for bit in range(nbits):
            info_copy(bit).wait_recv()
            for chunk in range(CHUNKS):
                block_copy(bit, chunk).wait_recv()
        for step in range(ROUNDS):
            slot = jnp.int32(0)
            for bit in range(nbits):
                slot = jnp.where(plan_ref[step, 0] == (1 << bit), jnp.int32(bit), slot)
            for chunk in range(CHUNKS):
                part = pl.ds(chunk * size, size)
                add_tile(slots[slot, part, :], infos[slot, :, part], F32(1.0 / (step + 1)))

    total = jnp.sum(mass[...], axis=1, keepdims=True)
    pull_total = jnp.sum(pulled[...], axis=1, keepdims=True)
    out_ref[...] = (acc[...] + own[...].astype(F32) * pull_total) / total

    for bit in range(nbits):
        info_copy(bit).wait_send()
        for chunk in range(CHUNKS):
            block_copy(bit, chunk).wait_send()


def per_device(particles, class_ids, score_table, precision, plan, median):
    rows, dims = particles.shape
    nbits = lax.axis_size("blk").bit_length() - 1
    vmem = pl.BlockSpec(memory_space=pltpu.VMEM)
    smem = pl.BlockSpec(memory_space=pltpu.SMEM)
    return pl.pallas_call(
        functools.partial(kernel, nbits),
        out_shape=jax.ShapeDtypeStruct((rows, dims), F32),
        in_specs=[smem, smem, pl.BlockSpec(memory_space=pl.ANY), vmem, vmem, vmem],
        out_specs=vmem,
        scratch_shapes=[
            pltpu.VMEM((rows, dims), BF16),
            pltpu.VMEM((nbits, rows, dims), BF16),
            pltpu.VMEM((8, rows), F32),
            pltpu.VMEM((nbits, 8, rows), F32),
            pltpu.VMEM((rows, 128), F32),
            pltpu.VMEM((3 * score_table.shape[0], dims), BF16),
            pltpu.VMEM((rows, dims), F32),
            pltpu.VMEM((rows, 128), F32),
            pltpu.VMEM((rows, 128), F32),
            pltpu.SemaphoreType.DMA,
            pltpu.SemaphoreType.DMA((nbits, CHUNKS)),
            pltpu.SemaphoreType.DMA((nbits, CHUNKS)),
            pltpu.SemaphoreType.DMA((nbits,)),
            pltpu.SemaphoreType.DMA((nbits,)),
        ],
        compiler_params=pltpu.CompilerParams(
            collective_id=0, has_side_effects=True, vmem_limit_bytes=32 * 1024 * 1024
        ),
        name="stein_drift",
    )(
        plan,
        median,
        particles,
        class_ids.reshape(1, rows),
        score_table,
        precision.reshape(1, dims),
    )


def solution(mesh):
    placed = (P(("groups", "blk"), None), P(("groups", "blk")), P(), P(), P(), P("groups"))
    return jax.shard_map(
        per_device,
        mesh=mesh,
        in_specs=placed,
        out_specs=P(("groups", "blk"), None),
        check_vma=False,
    )
```

time: 176 us -> 25.5 us (0.14)
  waiting for transfers between devices: 122 us -> 0 us
  starting transfers between devices: 31.5 us -> 0 us
  Pallas kernels: 0 us -> 21.3 us
  between operations: 11.2 us -> 0.7 us
  matrix products: 7.46 us -> 0 us
  other arithmetic: 2.2 us -> 0 us
  local copies, waits for them, and re-layouts: 1.49 us -> 3.26 us
    ppermute x26 -> x0, waiting for transfers between devices: 122 us -> none  [swapped(): lax.ppermute(array, axis, [(i, i ^ 1 << stride) for i in range(lax.axis_s...]
    ppermute x26 -> x0, starting transfers between devices: 31.5 us -> none  [swapped(): lax.ppermute(array, axis, [(i, i ^ 1 << stride) for i in range(lax.axis_s...]
    pallas_call x0 -> x1, Pallas kernels: none -> 21.3 us  [per_device(): pl.pallas_call(functools.partial(kernel, nbits), out_shape=jax.ShapeDtype...]
    dot_general x16 -> x0, matrix products: 7.46 us -> none  [the longest x5 2.3 us: tile_terms(): weighted = jnp.dot(kernel, right_scores, preferred_element_type=jnp.float32)]
    unnamed x6 -> x11, local copies, waits for them, and re-layouts: 0.91 us -> 3.26 us
  transfers between devices with their start and end apart: 26 -> 0, of which waited for: 14 -> 0; matrix products, arithmetic and copies ran while one was open for 5% -> 0% of each run, Pallas kernels for 0% -> 0%
where the time goes in v1:
time: 25.5 us; the launch traced here: 25.3 us
  Pallas kernels  21.3 us (84%)
  local copies, waits for them, and re-layouts  3.26 us (13%)
  between operations  0.7 us (3%)
    pallas_call x1, Pallas kernels, per_device(): pl.pallas_call(functools.partial(kernel, nbits), out_shape=jax.ShapeDtype...  21.3 us
    unnamed x11, local copies, waits for them, and re-layouts  3.26 us

profile of v1, /device:TPU:0, one launch (start us, length us, event | category | flops | bytes accessed | tf_op | source)
XLA Modules:
  0.0 25.3 jit_solution(7189378294944372245)
XLA Ops:
  0.0 0.0 copy-start.3
  0.7 0.0 copy-start.2
  0.7 0.0 copy-start.4
  0.7 0.0 copy-done.3
  0.7 0.7 %copy-done.2 = s32[4,16]{1,0:T(4,128)S(1)} copy-done((s32[4,16]{1,0:T(4,128)S(1)}, s32[4,16]{1,0:T(4,128)}, u32[]{:S(2)}) %copy-start.2) | copy-done | bytes 280
  1.4 0.0 copy-done.4
  1.4 0.0 copy-start
  1.4 0.9 %copy-done = bf16[512,256]{1,0:T(8,128)(2,1)S(1)} copy-done((bf16[512,256]{1,0:T(8,128)(2,1)S(1)}, bf16[512,256]{1,0:T(8,128)(2,1)}, u32[]{:S(2)}) %copy-start) | copy-done | bytes 262168
  2.3 0.0 copy-start.1
  2.3 0.8 %copy-done.1 = f32[64,256]{1,0:T(8,128)S(1)} copy-done((f32[64,256]{1,0:T(8,128)S(1)}, f32[64,256]{1,0:T(8,128)}, u32[]{:S(2)}) %copy-start.1) | copy-done | bytes 65560
  3.2 21.3 %stein_drift.1 = f32[512,256]{1,0:T(8,128)S(1)} custom-call(s32[4,16]{1,0:T(4,128)S(1)} %copy-done.2, f32[1]{0:T(128)S(6)} %copy.8.median_ref, bf16[512,256]{1,0:T(8,128)(2,1)S(1)} %copy-done, s32[1,512]{1,0:T(1,128)S(1)} %bitcast.2, f32[64,256]{1,0:T(8,128)S(1)} %copy-done.1, f32[1,256]{1,0:T(1,128)S(1)} %bitcast.3), custom_call_target="tpu_custom_call" | custom-call | tf_op jit(solution)/shard_map/stein_drift/pallas_call | solution.py:194
  24.5 0.8 %copy.9 = f32[512,256]{1,0:T(8,128)} copy(f32[512,256]{1,0:T(8,128)S(1)} %stein_drift.1) | data formatting | bytes 1048576
Async XLA Ops:
  0.0 0.7 %copy-start.3 = (s32[512]{0:T(512)S(1)}, s32[512]{0:T(512)}, u32[]{:S(2)}) copy-start(s32[512]{0:T(512)} %param.7) | copy-start | bytes 6148
  0.7 0.7 %copy-start.2 = (s32[4,16]{1,0:T(4,128)S(1)}, s32[4,16]{1,0:T(4,128)}, u32[]{:S(2)}) copy-start(s32[4,16]{1,0:T(4,128)} %plan_ref.1) | copy-start | bytes 772
  0.7 0.7 %copy-start.4 = (f32[256]{0:T(256)S(1)}, f32[256]{0:T(256)}, u32[]{:S(2)}) copy-start(f32[256]{0:T(256)} %param.9) | copy-start | bytes 3076
  1.4 0.9 %copy-start = (bf16[512,256]{1,0:T(8,128)(2,1)S(1)}, bf16[512,256]{1,0:T(8,128)(2,1)}, u32[]{:S(2)}) copy-start(bf16[512,256]{1,0:T(8,128)(2,1)} %x_hbm.1) | copy-start | bytes 786436
  2.3 0.8 %copy-start.1 = (f32[64,256]{1,0:T(8,128)S(1)}, f32[64,256]{1,0:T(8,128)}, u32[]{:S(2)}) copy-start(f32[64,256]{1,0:T(8,128)} %table_ref.1) | copy-start | bytes 196612

commit v2 on v1

v2 whole, which is shorter than its diff:
```python
import functools
import math

import jax
import jax.numpy as jnp
from jax import lax
from jax.experimental import pallas as pl
from jax.experimental.pallas import tpu as pltpu
from jax.sharding import PartitionSpec as P

ROUNDS = 4
CHUNKS = 4
LOG2E = math.log2(math.e)
F32, BF16 = jnp.float32, jnp.bfloat16


def flipped(index, bit):
    return index + (1 - 2 * ((index // (1 << bit)) % 2)) * (1 << bit)


def split_in_three(table):
    high = table.astype(BF16)
    rest = table - high.astype(F32)
    middle = rest.astype(BF16)
    low = (rest - middle.astype(F32)).astype(BF16)
    return jnp.concatenate([high, middle, low], axis=0)


def kernel(
    nbits,
    x_hbm,
    ids_hbm,
    table_hbm,
    prec_hbm,
    median_hbm,
    plan_hbm,
    out_ref,
    own,
    ids_ref,
    table_ref,
    prec_ref,
    median_ref,
    plan_ref,
    slots,
    own_info,
    infos,
    looked,
    norms,
    pieces,
    acc,
    mass,
    pulled,
    own_sem,
    send_sem,
    recv_sem,
    info_send,
    info_recv,
):
    rows, dims = own.shape
    size = rows // CHUNKS
    classes = table_ref.shape[0]
    me = lax.axis_index("blk")

    barrier = pltpu.get_barrier_semaphore()
    for bit in range(nbits):
        pl.semaphore_signal(
            barrier,
            inc=1,
            device_id={"blk": flipped(me, bit)},
            device_id_type=pl.DeviceIdType.MESH,
        )
    sources = (x_hbm, ids_hbm, table_hbm, prec_hbm, median_hbm, plan_hbm)
    copies = (own, ids_ref, table_ref, prec_ref, median_ref, plan_ref)
    loads = [
        pltpu.make_async_copy(source, copy, own_sem.at[place])
        for place, (source, copy) in enumerate(zip(sources, copies))
    ]
    for load in loads:
        load.start()
    for load in loads:
        load.wait()

    wide = own[...].astype(F32)
    half = 0.5 * jnp.sum(wide * wide, axis=1, keepdims=True)
    norms[...] = jnp.broadcast_to(half, norms.shape)
    half_row = jnp.transpose(norms[...])[0:2, :]
    ids_row = jnp.broadcast_to(ids_ref[...].astype(F32), half_row.shape)
    row = lax.broadcasted_iota(jnp.int32, half_row.shape, 0)
    own_info[...] = jnp.where(row == 0, ids_row, half_row)

    pl.semaphore_wait(barrier, nbits)

    def block_copy(bit, chunk):
        part = pl.ds(chunk * size, size)
        return pltpu.make_async_remote_copy(
            src_ref=x_hbm.at[part],
            dst_ref=slots.at[bit, part],
            send_sem=send_sem.at[bit, chunk],
            recv_sem=recv_sem.at[bit, chunk],
            device_id={"blk": flipped(me, bit)},
            device_id_type=pl.DeviceIdType.MESH,
        )

    def info_copy(bit):
        return pltpu.make_async_remote_copy(
            src_ref=own_info,
            dst_ref=infos.at[bit],
            send_sem=info_send.at[bit],
            recv_sem=info_recv.at[bit],
            device_id={"blk": flipped(me, bit)},
            device_id_type=pl.DeviceIdType.MESH,
        )

    for bit in reversed(range(nbits)):
        info_copy(bit).start()
    for chunk in range(CHUNKS):
        for bit in reversed(range(nbits)):
            block_copy(bit, chunk).start()
    pieces[...] = split_in_three(table_ref[...])
    acc[...] = jnp.zeros_like(acc)
    mass[...] = jnp.zeros_like(mass)
    pulled[...] = jnp.zeros_like(pulled)
    med = jnp.full((1, 1), median_ref[0], F32)
    inv_h = F32(math.log(1.0 + (ROUNDS + 1) * rows)) / (med * med)
    prec = prec_ref[...]

    def look_up(ids):
        number = lax.broadcasted_iota(jnp.int32, (classes, ids.shape[1]), 0).astype(F32)
        onehot = jnp.transpose((number == ids).astype(F32)).astype(BF16)
        return jnp.dot(
            jnp.concatenate([onehot, onehot, onehot], axis=1),
            pieces[...],
            preferred_element_type=F32,
        )

    def add_tile(right, offsets, half_right, share):
        count = right.shape[0]
        pull = (2.0 * inv_h) * share
        points = right.astype(F32)
        scores = (offsets - prec * points).astype(BF16).astype(F32)
        terms = (scores - jnp.broadcast_to(pull, (1, dims)) * points).astype(BF16)
        gram = lax.dot_general(
            own[...], right, (((1,), (1,)), ((), ())), preferred_element_type=F32
        )
        left_half = jnp.concatenate([norms[...]] * (count // 128), axis=1)
        scale = jnp.broadcast_to(pull * LOG2E, (1, count))
        weights = jnp.exp2(((gram - left_half) - half_right) * scale).astype(BF16)
        acc[...] += jnp.dot(weights, terms, preferred_element_type=F32)
        wide_weights = weights.astype(F32)
        part = wide_weights[:, :128]
        for lane in range(128, count, 128):
            part = part + wide_weights[:, lane : lane + 128]
        mass[...] += part
        pulled[...] += part * jnp.broadcast_to(pull, (1, 128))

    wide_size = rows // 2
    for half_block in range(2):
        part = pl.ds(half_block * wide_size, wide_size)
        add_tile(own[part, :], look_up(own_info[0:1, part]), own_info[1:2, part], F32(1.0))

    for bit in range(nbits):
        info_copy(bit).wait_recv()
        looked[bit] = look_up(infos[bit, 0:1, :])

    def add_part(slot, start, count, share):
        part = pl.ds(start, count)
        add_tile(slots[slot, part, :], looked[slot, part, :], infos[slot, 1:2, part], share)

    def share_of_bit(bit):
        share = F32(0.0)
        for step in range(ROUNDS):
            share = jnp.where(plan_ref[step, 0] == (1 << bit), F32(1.0 / (step + 1)), share)
        return share

    if nbits == ROUNDS:
        near = nbits // 2
        for bit in range(near):
            for half_block in range(2):
                for chunk in range(half_block * CHUNKS // 2, (half_block + 1) * CHUNKS // 2):
                    block_copy(bit, chunk).wait_recv()
                add_part(bit, half_block * wide_size, wide_size, share_of_bit(bit))
        for chunk in range(CHUNKS):
            for bit in reversed(range(near, nbits)):
                block_copy(bit, chunk).wait_recv()
                add_part(bit, chunk * size, size, share_of_bit(bit))
    else:
        for bit in range(nbits):
            for chunk in range(CHUNKS):
                block_copy(bit, chunk).wait_recv()
        for step in range(ROUNDS):
            slot = jnp.int32(0)
            for bit in range(nbits):
                slot = jnp.where(plan_ref[step, 0] == (1 << bit), jnp.int32(bit), slot)
            for half_block in range(2):
                add_part(slot, half_block * wide_size, wide_size, F32(1.0 / (step + 1)))

    scale = 1.0 / jnp.sum(mass[...], axis=1, keepdims=True)
    pull_total = jnp.sum(pulled[...], axis=1, keepdims=True)
    out_ref[...] = (acc[...] + own[...].astype(F32) * pull_total) * scale

    for bit in range(nbits):
        info_copy(bit).wait_send()
        for chunk in range(CHUNKS):
            block_copy(bit, chunk).wait_send()


def per_device(particles, class_ids, score_table, precision, plan, median):
    rows, dims = particles.shape
    nbits = lax.axis_size("blk").bit_length() - 1
    vmem = pl.BlockSpec(memory_space=pltpu.VMEM)
    hbm = pl.BlockSpec(memory_space=pltpu.HBM)
    return pl.pallas_call(
        functools.partial(kernel, nbits),
        out_shape=pltpu.VMEM((rows, dims), F32),
        in_specs=[hbm] * 6,
        out_specs=vmem,
        scratch_shapes=[
            pltpu.VMEM((rows, dims), BF16),
            pltpu.VMEM((1, rows), jnp.int32),
            pltpu.VMEM(score_table.shape, F32),
            pltpu.VMEM((1, dims), F32),
            pltpu.SMEM((1,), F32),
            pltpu.SMEM(plan.shape, jnp.int32),
            pltpu.VMEM((nbits, rows, dims), BF16),
            pltpu.VMEM((2, rows), F32),
            pltpu.VMEM((nbits, 2, rows), F32),
            pltpu.VMEM((nbits, rows, dims), F32),
            pltpu.VMEM((rows, 128), F32),
            pltpu.VMEM((3 * score_table.shape[0], dims), BF16),
            pltpu.VMEM((rows, dims), F32),
            pltpu.VMEM((rows, 128), F32),
            pltpu.VMEM((rows, 128), F32),
            pltpu.SemaphoreType.DMA((6,)),
            pltpu.SemaphoreType.DMA((nbits, CHUNKS)),
            pltpu.SemaphoreType.DMA((nbits, CHUNKS)),
            pltpu.SemaphoreType.DMA((nbits,)),
            pltpu.SemaphoreType.DMA((nbits,)),
        ],
        compiler_params=pltpu.CompilerParams(
            collective_id=0, has_side_effects=True, vmem_limit_bytes=60 * 1024 * 1024
        ),
        name="stein_drift",
    )(
        particles,
        class_ids.reshape(1, rows),
        score_table,
        precision.reshape(1, dims),
        median,
        plan,
    )


def solution(mesh):
    placed = (P(("groups", "blk"), None), P(("groups", "blk")), P(), P(), P(), P("groups"))
    return jax.shard_map(
        per_device,
        mesh=mesh,
        in_specs=placed,
        out_specs=P(("groups", "blk"), None),
        check_vma=False,
    )
```

time: 25.5 us -> 20.1 us (0.79)
  Pallas kernels: 21.3 us -> 18.5 us
  local copies, waits for them, and re-layouts: 3.26 us -> 0.8 us
    pallas_call x1, Pallas kernels: 21.3 us -> 18.5 us  [per_device(): pl.pallas_call(functools.partial(kernel, nbits), out_shape=pltpu.VMEM((ro...]
    unnamed x11 -> x1, local copies, waits for them, and re-layouts: 3.26 us -> 0.8 us
where the time goes in v2:
time: 20.1 us; the launch traced here: 19.9 us
  Pallas kernels  18.5 us (92%)
  local copies, waits for them, and re-layouts  0.8 us (4%)
  between operations  0.66 us (3%)
    pallas_call x1, Pallas kernels, per_device(): pl.pallas_call(functools.partial(kernel, nbits), out_shape=pltpu.VMEM((ro...  18.5 us
    unnamed x1, local copies, waits for them, and re-layouts  0.8 us

profile of v2, /device:TPU:0, one launch (start us, length us, event | category | flops | bytes accessed | tf_op | source)
XLA Modules:
  0.0 19.9 jit_solution(17623123059878334738)
XLA Ops:
  0.7 18.5 %stein_drift.1 = f32[512,256]{1,0:T(8,128)S(1)} custom-call(bf16[512,256]{1,0:T(8,128)(2,1)} %x_hbm.1, s32[1,512]{1,0:T(1,128)} %bitcast.2, f32[64,256]{1,0:T(8,128)} %table_hbm.1, f32[1,256]{1,0:T(1,128)} %bitcast.3, f32[1]{0:T(128)S(6)} %copy.9.median_hbm, s32[4,16]{1,0:T(4,128)} %plan_hbm.1), custom_call_target="tpu_custom_call" | custom-call | tf_op jit(solution)/shard_map/stein_drift/pallas_call | solution.py:212
  19.1 0.8 %copy.8 = f32[512,256]{1,0:T(8,128)} copy(f32[512,256]{1,0:T(8,128)S(1)} %stein_drift.1) | data formatting | bytes 1048576

commit v3 on v2

--- a/solution.py
+++ b/solution.py
@@ -114,7 +114,9 @@
     for bit in reversed(range(nbits)):
         info_copy(bit).start()
     for chunk in range(CHUNKS):
-        for bit in reversed(range(nbits)):
+        block_copy(nbits - 1, chunk).start()
+    for chunk in range(CHUNKS):
+        for bit in reversed(range(nbits - 1)):
             block_copy(bit, chunk).start()
     pieces[...] = split_in_three(table_ref[...])
     acc[...] = jnp.zeros_like(acc)
@@ -173,7 +175,7 @@
         return share
 
     if nbits == ROUNDS:
-        near = nbits // 2
+        near = nbits - 1
         for bit in range(near):
             for half_block in range(2):
                 for chunk in range(half_block * CHUNKS // 2, (half_block + 1) * CHUNKS // 2):

time: 20.1 us -> 20.1 us (level)
  no operation moved by 1% of the time
where the time goes in v3:
time: 20.1 us; the launch traced here: 20 us
  Pallas kernels  18.5 us (92%)
  local copies, waits for them, and re-layouts  0.8 us (4%)
  between operations  0.66 us (3%)
    pallas_call x1, Pallas kernels, per_device(): pl.pallas_call(functools.partial(kernel, nbits), out_shape=pltpu.VMEM((ro...  18.5 us
    unnamed x1, local copies, waits for them, and re-layouts  0.8 us

profile of v3, /device:TPU:0, one launch (start us, length us, event | category | flops | bytes accessed | tf_op | source)
XLA Modules:
  0.0 20.0 jit_solution(9718349060021170525)
XLA Ops:
  0.7 18.5 %stein_drift.1 = f32[512,256]{1,0:T(8,128)S(1)} custom-call(bf16[512,256]{1,0:T(8,128)(2,1)} %x_hbm.1, s32[1,512]{1,0:T(1,128)} %bitcast.2, f32[64,256]{1,0:T(8,128)} %table_hbm.1, f32[1,256]{1,0:T(1,128)} %bitcast.3, f32[1]{0:T(128)S(6)} %copy.9.median_hbm, s32[4,16]{1,0:T(4,128)} %plan_hbm.1), custom_call_target="tpu_custom_call" | custom-call | tf_op jit(solution)/shard_map/stein_drift/pallas_call | solution.py:214
  19.2 0.8 %copy.8 = f32[512,256]{1,0:T(8,128)} copy(f32[512,256]{1,0:T(8,128)S(1)} %stein_drift.1) | data formatting | bytes 1048576
